TPU v7x, 128 devices: a whole 4x4x4 slice. The times are simulated.
128 devices in a mesh: row: 16 (over x, y_lo, core), col: 8 (over z, y_hi).
Axes of the slice: x: 4, y: 4 (y_hi: 2, y_lo: 2; y = y_hi * 2 + y_lo), z: 4, core: 2. Of those that a mesh axis runs over, the one named last changes fastest.
Arguments:
- amplitudes: bfloat16 [24576, 24576], P('col', 'row'), may hold values from -0.0390625 to 0.0390625
- cholesky: bfloat16 [24576, 1280], P(('row', 'col')), may hold values from -5 to 5
- occ_map: int32 [24576], replicated, may hold values from 0 to 47
- vir_map: int32 [24576], replicated, may hold values from 0 to 511
Outputs:
- new_amplitudes: bfloat16 [24576, 24576], P('col', 'row')
All inputs are finite; a program needn't handle non-finite values.
Results may differ from a plain program's by a relative error of at most 0.0056.
Values may be sent and summed in bfloat16 or wider, within the bound.
A program may use at most 128 MiB of HBM per device.

v0:
```python
import jax
import jax.numpy as jnp
from jax import lax
from jax.sharding import PartitionSpec as P

NOCC = 48
NVIR = 512


def broadcast(x, axis, root):
    mine = lax.axis_index(axis) == root
    return lax.psum(jnp.where(mine, x, jnp.zeros_like(x)), axis)


def pair_gap(occ_map, vir_map):
    occ = occ_map.astype(jnp.float32)
    vir = vir_map.astype(jnp.float32)
    return 0.5 + 2.5 * jnp.sqrt(vir / NVIR) + (0.5 + 2.5 * occ / NOCC)


def body(amplitudes, cholesky, occ_map, vir_map):
    tile_rows, tile_cols = amplitudes.shape
    row_index = lax.axis_index("row")
    col_index = lax.axis_index("col")
    q_start = row_index * tile_cols
    p_start = col_index * tile_rows
    offset = q_start - p_start
    on_diag = jnp.logical_and(offset >= 0, offset < tile_rows).astype(jnp.float32)
    safe_offset = jnp.clip(offset, 0, tile_rows - tile_cols)
    piece = lax.all_gather(cholesky, "col", axis=0, tiled=True)
    count = piece.shape[0]
    total = jnp.dot(amplitudes, piece, preferred_element_type=jnp.float32)
    current = lax.dynamic_slice_in_dim(total, safe_offset, count, 0)
    partial_value = lax.dynamic_update_slice_in_dim(
        total, current + on_diag * piece.astype(jnp.float32), safe_offset, 0
    )
    y_block = lax.psum(partial_value, "row").astype(jnp.bfloat16)
    q_root = q_start // tile_rows
    q_inside = q_start % tile_rows
    own_part = lax.dynamic_slice_in_dim(y_block, q_inside, tile_cols, 0)
    y_cols = broadcast(own_part, "col", q_root)
    cycle = lax.dot_general(
        y_block, y_cols, (((1,), (1,)), ((), ())), preferred_element_type=jnp.float32
    )
    gap_rows = pair_gap(
        lax.dynamic_slice_in_dim(occ_map, p_start, tile_rows, 0),
        lax.dynamic_slice_in_dim(vir_map, p_start, tile_rows, 0),
    )
    gap_cols = pair_gap(
        lax.dynamic_slice_in_dim(occ_map, q_start, tile_cols, 0),
        lax.dynamic_slice_in_dim(vir_map, q_start, tile_cols, 0),
    )
    return (-cycle / (gap_rows[:, None] + gap_cols[None, :])).astype(jnp.bfloat16)


def solution(mesh):
    return jax.shard_map(
        body,
        mesh=mesh,
        in_specs=(P("col", "row"), P(("row", "col"), None), P(), P()),
        out_specs=P("col", "row"),
        check_vma=False,
    )
```

profile of v0, /device:TPU:1, one launch (start us, length us, event | category | flops | bytes accessed | tf_op | source)
XLA Modules:
  0.0 667.7 jit_solution(5515515563496372518)
XLA Ops:
  6.5 0.0 all-gather.2.cloned.1.call-start
  6.5 0.7 all-gather.2.cloned.1.call-update
  7.3 0.0 all-reduce.3.cloned.1.call-start
  7.4 74.6 %all-gather.2.cloned.1.call-done = bf16[1536,1280]{1,0:T(8,128)(2,1)} async-done(((bf16[192,1280]{1,0:T(8,128)(2,1)}), bf16[1536,1280]{1,0:T(8,128)(2,1)}) %all-gather.2.cloned.1.call-update) | async-done | bytes 3932176 | tf_op jit(solution)/shard_map/all_gather | solution.py:30
  81.9 16.7 %fusion = f32[3072,1280]{1,0:T(8,128)S(1)} fusion(bf16[3072,1536]{1,0:T(8,128)(2,1)} %param.4, bf16[1536,1280]{1,0:T(8,128)(2,1)} %all-gather.2.cloned.1.call-done), kind=kOutput, calls=%fused_computation.5 | convolution fusion | flops 12079595520 | bytes 29097984 | tf_op jit(solution)/shard_map/dot_general | solution.py:32
  98.6 0.0 copy-start
  98.6 5.5 copy-done
  104.1 6.7 %multiply_add_fusion = f32[1536,1280]{1,0:T(8,128)} fusion(bf16[1536,1280]{1,0:T(8,128)(2,1)} %all-gather.2.cloned.1.call-done, f32[3072,1280]{1,0:T(8,128)S(1)} %fusion, s32[]{:T(128)S(6)} %min.4, f32[]{:T(128)S(6)} %convert_element_type.24), kind=kLoop, calls=%fused_computation.1 | loop fusion | flops 5898240 | bytes 19660808 | tf_op jit(solution)/shard_map/add | solution.py:35
  110.9 19.0 %dynamic_update_slice.3 = f32[3072,1280]{1,0:T(8,128)} dynamic-update-slice(f32[3072,1280]{1,0:T(8,128)} %copy-done, f32[1536,1280]{1,0:T(8,128)} %multiply_add_fusion, s32[]{:T(128)S(6)} %min.4, s32[]{:T(128)} %constant.40.clone.1) | dynamic-update-slice | bytes 15728644 | tf_op jit(solution)/shard_map/dynamic_update_slice | solution.py:34
  129.8 334.6 %all-reduce.4 = bf16[3072,1280]{1,0:T(8,128)(2,1)} all-reduce(f32[3072,1280]{1,0:T(8,128)} %dynamic_update_slice.3), channel_id=1, replica_groups=mesh['row'=16,'col'=8] {'row'}, use_global_device_ids=true, to_apply=%region_0.1 | all-reduce | flops 3932160 | bytes 23592960 | tf_op jit(solution)/shard_map/psum | solution.py:37
  464.5 5.2 dynamic-slice_select_fusion
  469.7 0.0 all-reduce.3.cloned.1.call-update
  469.7 0.8 add_add_fusion.1
  470.5 0.7 add_add_fusion
  471.3 170.8 %all-reduce.3.cloned.1.call-done = bf16[1536,1280]{1,0:T(8,128)(2,1)} async-done(((bf16[1536,1280]{1,0:T(8,128)(2,1)}), bf16[1536,1280]{1,0:T(8,128)(2,1)}) %all-reduce.3.cloned.1.call-update) | async-done | bytes 3932176 | tf_op jit(solution)/shard_map/psum | solution.py:12
  642.1 18.7 %divide_convert_fusion = bf16[3072,1536]{1,0:T(8,128)(2,1)} fusion(bf16[3072,1280]{1,0:T(8,128)(2,1)} %all-reduce.4, bf16[1536,1280]{1,0:T(8,128)(2,1)} %all-reduce.3.cloned.1.call-done, f32[1536]{0:T(1024)S(1)} %add_add_fusion.1, f32[3072]{0:T(1024)S(1)} %add_add_fusion), kind=kOutput, calls=%fused_computation | convolution fusion | flops 12098469888 | bytes 21252096 | tf_op jit(solution)/shard_map/dot_general | solution.py:42
Async XLA Ops:
  6.5 75.4 %all-gather.2.cloned.1.call-start = ((), (), s32[]{:S(2)}) async-start(), calls=%async_computation | async-start | bytes 4423680 | tf_op jit(solution)/shard_map/all_gather | solution.py:30
  7.3 634.9 %all-reduce.3.cloned.1.call-start = ((), (), s32[]{:S(2)}) async-start(), calls=%async_computation.1 | async-start | bytes 7864320 | tf_op jit(solution)/shard_map/psum | solution.py:12
  98.6 5.5 copy-start
Sparse Core Ops, SparseCore 0:
  9.7 72.2 all-gather.1
  469.8 172.2 all-reduce.2
where the time goes:
time: 668 us
  blocking collectives  335 us (50%)
  waiting for transfers between devices  246 us (37%)
  matrix products  35.4 us (5%)
  local copies, waits for them, and re-layouts  24.5 us (4%)
  other arithmetic  13.5 us (2%)
  between operations  13.5 us (2%)
    psum x1, blocking collectives, body(): y_block = lax.psum(partial_value, 'row').astype(jnp.bfloat16)  335 us
    psum x1, waiting for transfers between devices, broadcast(): return lax.psum(jnp.where(mine, x, jnp.zeros_like(x)), axis)  171 us
    all_gather x1, waiting for transfers between devices, body(): piece = lax.all_gather(cholesky, 'col', axis=0, tiled=True)  74.6 us
    dynamic_update_slice x1, local copies, waits for them, and re-layouts, body(): lax.dynamic_update_slice_in_dim(total, current + on_diag * piece.astype(j...  19 us
    dot_general x1, matrix products, body(): lax.dot_general(y_block, y_cols, (((1,), (1,)), ((), ())), preferred_elem...  18.7 us
    dot_general x1, matrix products, body(): total = jnp.dot(amplitudes, piece, preferred_element_type=jnp.float32)  16.7 us
  transfers between devices with their start and end apart: 2, of which 2 were waited for; matrix products, arithmetic and copies ran while one was open for 0% of the time, Pallas kernels for 0%

commit v1 on v0

--- a/solution.py
+++ b/solution.py
@@ -9,7 +9,7 @@
 
 def broadcast(x, axis, root):
     mine = lax.axis_index(axis) == root
-    return lax.psum(jnp.where(mine, x, jnp.zeros_like(x)), axis)
+    return jnp.sum(lax.all_gather(jnp.where(mine, x, jnp.zeros_like(x)), axis), axis=0)
 
 
 def pair_gap(occ_map, vir_map):

time: 668 us -> 822 us (1.23)
  waiting for transfers between devices: 246 us -> 386 us
  other arithmetic: 13.5 us -> 27.1 us
    all_gather x0 -> x1, waiting for transfers between devices: none -> 311 us  [broadcast(): lax.all_gather(jnp.where(mine, x, jnp.zeros_like(x)), axis)]
    psum x1 -> x0, waiting for transfers between devices: 171 us -> none  [broadcast(): return lax.psum(jnp.where(mine, x, jnp.zeros_like(x)), axis)]
    reduce_sum x0 -> x1, other arithmetic: none -> 13.6 us  [broadcast(): jnp.sum(lax.all_gather(jnp.where(mine, x, jnp.zeros_like(x)), axis), axis=0)]
where the time goes in v1:
time: 822 us; the launch traced here: 821 us
  waiting for transfers between devices  386 us (47%)
  blocking collectives  335 us (41%)
  matrix products  35.4 us (4%)
  other arithmetic  27.1 us (3%)
  local copies, waits for them, and re-layouts  24.5 us (3%)
  between operations  13.5 us (2%)
    psum x1, blocking collectives, body(): y_block = lax.psum(partial_value, 'row').astype(jnp.bfloat16)  335 us
    all_gather x1, waiting for transfers between devices, broadcast(): lax.all_gather(jnp.where(mine, x, jnp.zeros_like(x)), axis)  311 us
    all_gather x1, waiting for transfers between devices, body(): piece = lax.all_gather(cholesky, 'col', axis=0, tiled=True)  74.6 us
    dynamic_update_slice x1, local copies, waits for them, and re-layouts, body(): lax.dynamic_update_slice_in_dim(total, current + on_diag * piece.astype(j...  19 us
    dot_general x1, matrix products, body(): lax.dot_general(y_block, y_cols, (((1,), (1,)), ((), ())), preferred_elem...  18.7 us
    dot_general x1, matrix products, body(): total = jnp.dot(amplitudes, piece, preferred_element_type=jnp.float32)  16.7 us
  transfers between devices with their start and end apart: 2, of which 2 were waited for; matrix products, arithmetic and copies ran while one was open for 0% of the time, Pallas kernels for 0%

profile of v1, /device:TPU:1, one launch (start us, length us, event | category | flops | bytes accessed | tf_op | source)
XLA Modules:
  0.0 821.1 jit_solution(5353700594664355159)
XLA Ops:
  6.5 0.0 all-gather.4.cloned.1.call-start
  6.5 0.7 all-gather.4.cloned.1.call-update
  7.3 0.0 all-gather.6.cloned.1.call-start
  7.4 74.6 %all-gather.4.cloned.1.call-done = bf16[1536,1280]{1,0:T(8,128)(2,1)} async-done(((bf16[192,1280]{1,0:T(8,128)(2,1)}), bf16[1536,1280]{1,0:T(8,128)(2,1)}) %all-gather.4.cloned.1.call-update) | async-done | bytes 3932176 | tf_op jit(solution)/shard_map/all_gather | solution.py:30
  81.9 16.7 %fusion = f32[3072,1280]{1,0:T(8,128)S(1)} fusion(bf16[3072,1536]{1,0:T(8,128)(2,1)} %param.4, bf16[1536,1280]{1,0:T(8,128)(2,1)} %all-gather.4.cloned.1.call-done), kind=kOutput, calls=%fused_computation.5 | convolution fusion | flops 12079595520 | bytes 29097984 | tf_op jit(solution)/shard_map/dot_general | solution.py:32
  98.6 0.0 copy-start
  98.6 5.5 copy-done
  104.1 6.7 multiply_add_fusion
  110.9 19.0 %dynamic_update_slice.3 = f32[3072,1280]{1,0:T(8,128)} dynamic-update-slice(f32[3072,1280]{1,0:T(8,128)} %copy-done, f32[1536,1280]{1,0:T(8,128)} %multiply_add_fusion, s32[]{:T(128)S(6)} %min.4, s32[]{:T(128)} %constant.42.clone.1) | dynamic-update-slice | bytes 15728644 | tf_op jit(solution)/shard_map/dynamic_update_slice | solution.py:34
  129.8 334.7 %all-reduce.1 = bf16[3072,1280]{1,0:T(8,128)(2,1)} all-reduce(f32[3072,1280]{1,0:T(8,128)} %dynamic_update_slice.3), channel_id=1, replica_groups=mesh['row'=16,'col'=8] {'row'}, use_global_device_ids=true, to_apply=%region_0.1 | all-reduce | flops 3932160 | bytes 23592960 | tf_op jit(solution)/shard_map/psum | solution.py:37
  464.5 5.2 dynamic-slice_select_fusion
  469.7 0.0 all-gather.6.cloned.1.call-update
  469.7 0.8 add_add_fusion.1
  470.5 0.7 add_add_fusion
  471.3 310.6 %all-gather.6.cloned.1.call-done = bf16[12288,1280]{1,0:T(8,128)(2,1)} async-done(((bf16[1536,1280]{1,0:T(8,128)(2,1)}), bf16[12288,1280]{1,0:T(8,128)(2,1)}) %all-gather.6.cloned.1.call-update) | async-done | bytes 31457296 | tf_op jit(solution)/shard_map/all_gather | solution.py:12
  781.9 13.6 %reduce_sum.12 = bf16[1536,1280]{1,0:T(8,128)(2,1)} reduce(bf16[8,1536,1280]{2,1,0:T(8,128)(2,1)} %bitcast.5, bf16[]{:T(256)} %constant.49.clone.1), dimensions={0}, to_apply=%region_1.2 | reduce | flops 13762560 | bytes 35389440 | tf_op jit(solution)/shard_map/reduce_sum | solution.py:12
  795.5 18.7 %divide_convert_fusion = bf16[3072,1536]{1,0:T(8,128)(2,1)} fusion(bf16[3072,1280]{1,0:T(8,128)(2,1)} %all-reduce.1, bf16[1536,1280]{1,0:T(8,128)(2,1)} %reduce_sum.12, f32[1536]{0:T(1024)S(1)} %add_add_fusion.1, f32[3072]{0:T(1024)S(1)} %add_add_fusion), kind=kOutput, calls=%fused_computation | convolution fusion | flops 12098469888 | bytes 21252096 | tf_op jit(solution)/shard_map/dot_general | solution.py:42
Async XLA Ops:
  6.5 75.4 %all-gather.4.cloned.1.call-start = ((), (), s32[]{:S(2)}) async-start(), calls=%async_computation | async-start | bytes 4423680 | tf_op jit(solution)/shard_map/all_gather | solution.py:30
  7.3 774.6 %all-gather.6.cloned.1.call-start = ((), (), s32[]{:S(2)}) async-start(), calls=%async_computation.1 | async-start | bytes 35389440 | tf_op jit(solution)/shard_map/all_gather | solution.py:12
  98.6 5.5 copy-start
Sparse Core Ops, SparseCore 0:
  9.7 72.2 all-gather.3
  469.8 312.0 all-gather.5
